TPU v7x, 256 devices: a whole 4x4x8 slice. The times are simulated.
256 devices in a mesh: doc: 8 (over z_lo, core), layer: 32 (over y, x, z_hi).
Axes of the slice: x: 4, y: 4, z: 8 (z_hi: 2, z_lo: 4; z = z_hi * 4 + z_lo), core: 2. Of those that a mesh axis runs over, the one named last changes fastest.
Arguments:
- query_grads: bfloat16 [32, 256, 4096], P('layer', 'doc'), may hold values from -6 to 6
- doc_grads: bfloat16 [32, 8192, 4096], P('layer', 'doc'), may hold values from -6 to 6
- inverse: bfloat16 [32, 4096, 4096], P('layer', None, 'doc'), may hold values from -1 to 2
Outputs:
- scores: float32 [8192, 256], P(('doc', 'layer'))
All inputs are finite; a program needn't handle non-finite values.
Results may differ from a plain program's by a relative error of at most 0.0029.
Values may be sent and summed in bfloat16 or wider, within the bound.
A program may use at most 64 MiB of HBM per device.

v0:
```python
import math

import jax
import jax.numpy as jnp
from jax import lax
from jax.sharding import PartitionSpec as P

F = 4096


def against(documents, precond):
    return lax.dot_general(
        documents, precond, (((1,), (1,)), ((), ())), preferred_element_type=jnp.float32
    )


def per_device(query_grads, doc_grads, inverse):
    queries = query_grads[0]
    documents = doc_grads[0]
    column_block = inverse[0]
    layers = lax.axis_size("layer")
    factor = 1.0 / math.sqrt(F * layers)
    pre_block = jnp.dot(
        lax.all_gather(queries, "doc", axis=0, tiled=True),
        column_block,
        preferred_element_type=jnp.float32,
    ).astype(jnp.bfloat16)
    precond = lax.all_gather(pre_block, "doc", axis=1, tiled=True)
    own = lax.psum_scatter(against(documents, precond), "layer", scatter_dimension=0, tiled=True)
    return own * factor


def solution(mesh):
    in_specs = (P("layer", "doc", None), P("layer", "doc", None), P("layer", None, "doc"))
    out_specs = P(("doc", "layer"), None)
    return jax.shard_map(
        per_device, mesh=mesh, in_specs=in_specs, out_specs=out_specs, check_vma=False
    )
```

profile of v0, /device:TPU:32, one launch (start us, length us, event | category | flops | bytes accessed | tf_op | source)
XLA Modules:
  0.0 336.8 jit_solution(16771338661292083631)
XLA Ops:
  6.5 0.0 all-gather.6.cloned.1.call-start
  6.5 0.7 all-gather.6.cloned.1.call-update
  7.3 0.0 all-gather.4.cloned.1.call-start
  7.3 40.8 %all-gather.6.cloned.1.call-done = bf16[1,256,4096]{2,1,0:T(8,128)(2,1)} async-done(((bf16[1,32,4096]{2,1,0:T(8,128)(2,1)}), bf16[1,256,4096]{2,1,0:T(8,128)(2,1)}) %all-gather.6.cloned.1.call-update) | async-done | bytes 2097168 | tf_op jit(solution)/shard_map/all_gather | solution.py:24
  48.1 4.8 %fusion.8 = bf16[256,512]{1,0:T(8,128)(2,1)} fusion(bf16[1,4096,512]{2,1,0:T(8,128)(2,1)} %param.5, bf16[1,256,4096]{2,1,0:T(8,128)(2,1)} %all-gather.6.cloned.1.call-done), kind=kOutput, calls=%fused_computation.6 | convolution fusion | flops 1073872896 | bytes 6553600 | tf_op jit(solution)/shard_map/dot_general | solution.py:23
  52.9 0.0 all-gather.4.cloned.1.call-update
  52.9 0.0 reduce-scatter.4.cloned.1.call-start
  53.0 38.7 %all-gather.4.cloned.1.call-done = bf16[256,4096]{1,0:T(8,128)(2,1)} async-done(((bf16[256,512]{1,0:T(8,128)(2,1)}), bf16[256,4096]{1,0:T(8,128)(2,1)}) %all-gather.4.cloned.1.call-update) | async-done | bytes 2097168 | tf_op jit(solution)/shard_map/all_gather | solution.py:28
  91.6 6.4 %fusion.5 = f32[1024,256]{0,1:T(8,128)S(1)} fusion(bf16[256,4096]{1,0:T(8,128)(2,1)} %all-gather.4.cloned.1.call-done, bf16[1,1024,4096]{2,1,0:T(8,128)(2,1)} %param.4), kind=kOutput, calls=%fused_computation.5 | convolution fusion | flops 2147483648 | bytes 11534336 | tf_op jit(solution)/shard_map/dot_general | solution.py:12
  98.0 1.3 copy.7
  99.3 0.0 reduce-scatter.4.cloned.1.call-update
  99.4 229.5 %reduce-scatter.4.cloned.1.call-done = f32[32,256]{1,0:T(8,128)} async-done(((f32[1024,256]{1,0:T(8,128)}), f32[32,256]{1,0:T(8,128)}) %reduce-scatter.4.cloned.1.call-update) | async-done | bytes 32784 | tf_op jit(solution)/shard_map/reduce_scatter | solution.py:29
  328.8 1.4 broadcast_multiply_fusion
Async XLA Ops:
  6.5 41.6 %all-gather.6.cloned.1.call-start = ((), (), s32[]{:S(2)}) async-start(), calls=%async_computation.2 | async-start | bytes 2359296 | tf_op jit(solution)/shard_map/all_gather | solution.py:24
  7.3 84.4 %all-gather.4.cloned.1.call-start = ((), (), s32[]{:S(2)}) async-start(), calls=%async_computation.1 | async-start | bytes 2359296 | tf_op jit(solution)/shard_map/all_gather | solution.py:28
  52.9 275.9 %reduce-scatter.4.cloned.1.call-start = ((), (), s32[]{:S(2)}) async-start(), calls=%async_computation.3 | async-start | bytes 1081344 | tf_op jit(solution)/shard_map/reduce_scatter | solution.py:29
Sparse Core Ops, SparseCore 0:
  9.1 38.9 all-gather.5
  53.0 38.5 all-gather.3
  99.5 229.3 reduce-scatter.3
where the time goes:
time: 337 us
  waiting for transfers between devices  310 us (92%)
  between operations  13.1 us (4%)
  matrix products  11.1 us (3%)
    reduce_scatter x1, waiting for transfers between devices, per_device(): lax.psum_scatter(against(documents, precond), 'layer', scatter_dimension=...  229 us
    all_gather x1, waiting for transfers between devices, per_device(): lax.all_gather(queries, 'doc', axis=0, tiled=True)  40.8 us
    all_gather x1, waiting for transfers between devices, per_device(): precond = lax.all_gather(pre_block, 'doc', axis=1, tiled=True)  38.7 us
  transfers between devices with their start and end apart: 3, of which 3 were waited for; matrix products, arithmetic and copies ran while one was open for 0% of the time, Pallas kernels for 0%

commit v1 on v0

v1 whole, which is shorter than its diff:
```python
import math

import jax
import jax.numpy as jnp
from jax import lax
from jax.experimental import pallas as pl
from jax.experimental.pallas import tpu as pltpu
from jax.sharding import PartitionSpec as P

F = 4096
LAYERS = 32
Q = 256
ROWS = 1024
BATCH = 64
HALF = 128
COLS = 512
PIECES = 4
WIDE = F // PIECES
BLOCK = 64
MESH = pl.DeviceIdType.MESH
NT = (((1,), (1,)), ((), ()))


def kernel(
    q_hbm, docs_hbm, inv_hbm, o_ref,
    q_buf, inv_buf, docs_buf, p_buf, acc, own, sbuf, rbuf, total, zbuf,
    in_sem, q_send, q_recv, qs_send, qs_recv, p_send, p_recv, ps_send, ps_recv,
    r_send, r_recv, z_send, z_recv,
):
    d, l = lax.axis_index("doc"), lax.axis_index("layer")
    z, c = d // 2, d % 2
    y, x, h = l // 8, (l // 2) % 4, l % 2
    plane = y * 4 + x
    mid = ((z + 1) // 2) % 2
    outer = z + 1 - 2 * (z % 2)
    second = 2 - z // 2
    partner = (d, l + 1 - 2 * h)
    sibling = (z * 2 + 1 - c, l)

    def peer(i):
        return (d, ((y + i // 4) % 4) * 8 + ((x + i % 4) % 4) * 2 + h)

    def source(k):
        return jnp.where(k == 0, z, jnp.where(k == 1, outer, jnp.where(k == 2, (z + 2) % 4, 3 - z)))

    def remote(src, dst, ss, rs, to):
        return pltpu.make_async_remote_copy(
            src_ref=src, dst_ref=dst, send_sem=ss, recv_sem=rs, device_id=to, device_id_type=MESH
        )

    mine = pl.ds(pl.multiple_of(c * 32, 32), 32)
    q_in = [
        pltpu.make_async_copy(
            q_hbm.at[:, pl.ds(p * WIDE, WIDE)], q_buf.at[z, p, mine, :], in_sem.at[p]
        )
        for p in range(PIECES)
    ]
    inv_in = pltpu.make_async_copy(inv_hbm, inv_buf, in_sem.at[PIECES])
    docs_in = pltpu.make_async_copy(docs_hbm, docs_buf, in_sem.at[PIECES + 1])
    for copy in q_in:
        copy.start()
    inv_in.start()
    docs_in.start()

    barrier = pltpu.get_barrier_semaphore()
    for k in range(1, 4):
        pl.semaphore_signal(barrier, inc=1, device_id=(source(k) * 2 + c, l), device_id_type=MESH)
    pl.semaphore_signal(barrier, inc=1, device_id=sibling, device_id_type=MESH)
    pl.semaphore_signal(barrier, inc=1, device_id=partner, device_id_type=MESH)

    def greet(i, _):
        pl.semaphore_signal(barrier, inc=1, device_id=peer(i), device_id_type=MESH)
        return 0

    lax.fori_loop(1, 16, greet, 0)
    pl.semaphore_wait(barrier, 20)

    def q_copy(k, p, slot, at_k, to):
        piece = q_buf.at[source(k), p, mine, :]
        return remote(piece, piece, q_send.at[slot, p], q_recv.at[at_k - 1, p], (to * 2 + c, l))

    def q_share(k):
        piece = q_buf.at[source(k), :, mine, :]
        return remote(piece, piece, qs_send.at[k], qs_recv.at[k], sibling)

    for p in range(PIECES):
        q_in[p].wait()
        q_copy(0, p, 0, 1, outer).start()
        q_copy(0, p, 1, 2 + mid, second).start()
    q_share(0).start()

    def place(s):
        return 1 - (s + s // 2) % 2, s // 2

    def p_ref(half, s, core, j):
        return p_buf.at[half, s, core, pl.ds(pl.multiple_of(j * BATCH, BATCH), BATCH), :]

    def p_copy(k, half, j, slot, at_k, to):
        piece = p_ref(half, source(k), c, j)
        return remote(piece, piece, p_send.at[slot, half, j], p_recv.at[at_k - 1, half, j], (to * 2 + c, l))

    def p_share(k, half, j):
        piece = p_ref(half, source(k), c, j)
        return remote(piece, piece, ps_send.at[k, half, j], ps_recv.at[k, half, j], sibling)

    def precondition(k):
        q_share(k).wait_recv()
        s = source(k)
        pre = jnp.dot(q_buf[s, 0], inv_buf[pl.ds(0, WIDE), :], preferred_element_type=jnp.float32)
        for p in range(1, PIECES):
            pre += jnp.dot(
                q_buf[s, p], inv_buf[pl.ds(p * WIDE, WIDE), :], preferred_element_type=jnp.float32
            )
        half, j = place(s)
        p_buf[half, z, c, pl.ds(pl.multiple_of(j * BATCH, BATCH), BATCH), :] = pre.astype(jnp.bfloat16)

    def spread(k):
        half, j = place(source(k))
        p_copy(0, half, j, 0, 1, outer).start()
        p_copy(0, half, j, 1, 2 + mid, second).start()
        p_share(0, half, j).start()

    inv_in.wait()
    precondition(0)

    @pl.when(mid == 1)
    def _():
        def relay(p, _):
            for k in (3, 2):
                q_copy(k, p, 0, k, outer).wait_recv()
                q_copy(k, p, k, 5 - k, outer).start()
            return 0

        lax.fori_loop(0, PIECES, relay, 0)

    spread(0)

    def gather(step, _):
        k = (step + 2 * mid) % 3 + 1

        @pl.when((mid == 0) | (k == 1))
        def _():
            for p in range(PIECES):
                q_copy(k, p, 0, k, outer).wait_recv()

        q_share(k).start()
        precondition(k)
        spread(k)
        return 0

    lax.fori_loop(0, 3, gather, 0)

    docs_in.wait()

    def score(half, k):
        for j in range(2):
            p_share(k, half, j).wait_recv()
        s = source(k)
        part = 0.0
        for core in range(2):
            columns = pl.ds(pl.multiple_of(s * 2 * COLS + core * COLS, COLS), COLS)
            part += lax.dot_general(
                docs_buf[:, columns], p_buf[half, s, core], NT, preferred_element_type=jnp.float32
            )
        return part

    def sum_copy(half, i):
        return remote(
            sbuf.at[half, ((y + i // 4) % 4) * 4 + (x + i % 4) % 4], rbuf.at[half, i - 1],
            r_send.at[half, i - 1], r_recv.at[half, i - 1], peer(i),
        )

    def last_copy(half):
        rows = pl.ds(pl.multiple_of((1 - h) * 32, 32), 32)
        return remote(
            total.at[half, rows, :], zbuf.at[half], z_send.at[half], z_recv.at[half], partner
        )

    def collect(half):
        def add(i, running):
            sum_copy(half, i).wait_recv()
            return running + rbuf[half, i - 1].astype(jnp.float32)

        total[half] = lax.fori_loop(1, 16, add, own[half])
        last_copy(half).start()

    for half in range(2):
        acc[...] = score(half, 0)

        def step(i, _, half=half):
            k = jnp.where(mid == 1, 3 - i, 1 + i)
            for j in range(2):
                p_copy(k, half, j, 0, k, outer).wait_recv()

                @pl.when((mid == 1) & (i < 2))
                def _():
                    p_copy(k, half, j, k, 5 - k, outer).start()

                p_share(k, half, j).start()
            acc[...] += score(half, k)
            return 0

        if half == 0:
            lax.fori_loop(0, 3, step, 0)
        else:
            lax.fori_loop(0, 2, step, 0)
            collect(0)
            lax.fori_loop(2, 3, step, 0)
        for block in range(16):
            sbuf[half, block] = acc[pl.ds(block * BLOCK, BLOCK), :].astype(jnp.bfloat16)
        own[half] = acc[pl.ds(pl.multiple_of(plane * BLOCK, BLOCK), BLOCK), :]

        def send(i, _, half=half):
            sum_copy(half, i).start()
            return 0

        lax.fori_loop(1, 16, send, 0)

    collect(1)
    for half in range(2):
        last_copy(half).wait_recv()
        rows = pl.ds(pl.multiple_of(h * 32, 32), 32)
        o_ref[:, pl.ds(half * HALF, HALF)] = total[half, rows, :] + zbuf[half]

    for p in range(PIECES):
        q_copy(0, p, 0, 1, outer).wait_send()
        q_copy(0, p, 1, 2 + mid, second).wait_send()
    for half in range(2):
        for j in range(2):
            p_copy(0, half, j, 0, 1, outer).wait_send()
            p_copy(0, half, j, 1, 2 + mid, second).wait_send()

    @pl.when(mid == 1)
    def _():
        for k in (3, 2):
            for p in range(PIECES):
                q_copy(k, p, k, 5 - k, outer).wait_send()
            for half in range(2):
                for j in range(2):
                    p_copy(k, half, j, k, 5 - k, outer).wait_send()

    def shared(k, _):
        q_share(k).wait_send()
        for half in range(2):
            for j in range(2):
                p_share(k, half, j).wait_send()
        return 0

    lax.fori_loop(0, 4, shared, 0)

    def sent(i, _):
        sum_copy(0, i).wait_send()
        sum_copy(1, i).wait_send()
        return 0

    lax.fori_loop(1, 16, sent, 0)
    for half in range(2):
        last_copy(half).wait_send()


def per_device(query_grads, doc_grads, inverse):
    dma = pltpu.SemaphoreType.DMA
    bf16, f32 = jnp.bfloat16, jnp.float32
    out = pl.pallas_call(
        kernel,
        out_shape=jax.ShapeDtypeStruct((32, Q), f32),
        in_specs=[pl.BlockSpec(memory_space=pl.ANY)] * 3,
        out_specs=pl.BlockSpec(memory_space=pltpu.VMEM),
        scratch_shapes=[
            pltpu.VMEM((4, PIECES, BATCH, WIDE), bf16),
            pltpu.VMEM((F, COLS), bf16),
            pltpu.VMEM((ROWS, F), bf16),
            pltpu.VMEM((2, 4, 2, HALF, COLS), bf16),
            pltpu.VMEM((ROWS, HALF), f32),
            pltpu.VMEM((2, BLOCK, HALF), f32),
            pltpu.VMEM((2, 16, BLOCK, HALF), bf16),
            pltpu.VMEM((2, 15, BLOCK, HALF), bf16),
            pltpu.VMEM((2, BLOCK, HALF), f32),
            pltpu.VMEM((2, 32, HALF), f32),
            dma((PIECES + 2,)),
            dma((4, PIECES)),
            dma((3, PIECES)),
            dma((4,)),
            dma((4,)),
            dma((4, 2, 2)),
            dma((3, 2, 2)),
            dma((4, 2, 2)),
            dma((4, 2, 2)),
            dma((2, 15)),
            dma((2, 15)),
            dma((2,)),
            dma((2,)),
        ],
        compiler_params=pltpu.CompilerParams(
            collective_id=0, has_side_effects=True, vmem_limit_bytes=60 * 2**20
        ),
        name="scores",
    )(query_grads[0], doc_grads[0], inverse[0])
    factor = 1.0 / math.sqrt(F * LAYERS)
    return jnp.concatenate([out[:, 128:192], out[:, :128], out[:, 192:]], axis=1) * factor


def solution(mesh):
    in_specs = (P("layer", "doc", None), P("layer", "doc", None), P("layer", None, "doc"))
    out_specs = P(("doc", "layer"), None)
    return jax.shard_map(
        per_device, mesh=mesh, in_specs=in_specs, out_specs=out_specs, check_vma=False
    )
```

time: 337 us -> 65 us (0.19)
  the two profiles are of different devices: /device:TPU:32 before, /device:TPU:1 now
where the time goes in v1:
time: 65 us; the launch traced here: 64.8 us
  Pallas kernels  62.5 us (96%)
  local copies, waits for them, and re-layouts  1.59 us (2%)
  other arithmetic  0.7 us (1%)
    pallas_call x1, Pallas kernels, per_device(): pl.pallas_call(kernel, out_shape=jax.ShapeDtypeStruct((32, Q), f32), in_s...  62.5 us

profile of v1, /device:TPU:1, one launch (start us, length us, event | category | flops | bytes accessed | tf_op | source)
XLA Modules:
  0.0 64.8 jit_solution(8126268705104313695)
XLA Ops:
  0.0 62.5 %scores.1 = f32[32,256]{1,0:T(8,128)} custom-call(bf16[32,4096]{1,0:T(8,128)(2,1)} %bitcast.5, bf16[1024,4096]{1,0:T(8,128)(2,1)} %bitcast.3, bf16[4096,512]{1,0:T(8,128)(2,1)} %bitcast.4), custom_call_target="tpu_custom_call" | custom-call | tf_op jit(solution)/shard_map/scores/pallas_call | solution.py:264
  62.5 0.9 %fusion = (f32[32,64]{1,0:T(8,128)S(1)}, f32[32,64]{1,0:T(8,128)S(1)}) fusion(f32[32,256]{1,0:T(8,128)} %scores.1), kind=kLoop, calls=%fused_computation.1 | loop fusion | bytes 32768 | tf_op jit(solution)/shard_map/slice | solution.py:300
  63.4 0.7 %slice.10 = f32[32,128]{1,0:T(8,128)S(1)} slice(f32[32,256]{1,0:T(8,128)} %scores.1), slice={[0:32], [0:128]} | slice | bytes 32768 | tf_op jit(solution)/shard_map/slice | solution.py:300
  64.1 0.7 %maximum_multiply_fusion = f32[32,256]{1,0:T(8,128)} fusion(f32[32,64]{1,0:T(8,128)S(1)} %get-tuple-element.6, f32[32,128]{1,0:T(8,128)S(1)} %slice.10, f32[32,64]{1,0:T(8,128)S(1)} %get-tuple-element.5), kind=kLoop, calls=%fused_computation | loop fusion | flops 24576 | bytes 65536 | tf_op jit(solution)/shard_map/mul | solution.py:300

commit v2 on v1

--- a/solution.py
+++ b/solution.py
@@ -25,7 +25,7 @@
     q_hbm, docs_hbm, inv_hbm, o_ref,
     q_buf, inv_buf, docs_buf, p_buf, acc, own, sbuf, rbuf, total, zbuf,
     in_sem, q_send, q_recv, qs_send, qs_recv, p_send, p_recv, ps_send, ps_recv,
-    r_send, r_recv, z_send, z_recv,
+    r_send, r_recv, z_send, z_recv, line_sem, plane_sem,
 ):
     d, l = lax.axis_index("doc"), lax.axis_index("layer")
     z, c = d // 2, d % 2
@@ -59,21 +59,27 @@
     docs_in = pltpu.make_async_copy(docs_hbm, docs_buf, in_sem.at[PIECES + 1])
     for copy in q_in:
         copy.start()
-    inv_in.start()
-    docs_in.start()
 
     barrier = pltpu.get_barrier_semaphore()
-    for k in range(1, 4):
-        pl.semaphore_signal(barrier, inc=1, device_id=(source(k) * 2 + c, l), device_id_type=MESH)
-    pl.semaphore_signal(barrier, inc=1, device_id=sibling, device_id_type=MESH)
-    pl.semaphore_signal(barrier, inc=1, device_id=partner, device_id_type=MESH)
-
-    def greet(i, _):
-        pl.semaphore_signal(barrier, inc=1, device_id=peer(i), device_id_type=MESH)
-        return 0
-
-    lax.fori_loop(1, 16, greet, 0)
-    pl.semaphore_wait(barrier, 20)
+
+    def greet(to):
+        pl.semaphore_signal(barrier, inc=1, device_id=to, device_id_type=MESH)
+
+    def tell(semaphore):
+        pl.semaphore_signal(semaphore, inc=1, device_id=sibling, device_id_type=MESH)
+
+    @pl.when(c == 0)
+    def _():
+        for k in (2, 3, 1):
+            greet((source(k) * 2, l))
+        pl.semaphore_wait(barrier, 7)
+        tell(line_sem)
+
+    @pl.when(c == 1)
+    def _():
+        for k in (2, 3, 1, 0):
+            greet((source(k) * 2, l))
+        pl.semaphore_wait(line_sem, 1)
 
     def q_copy(k, p, slot, at_k, to):
         piece = q_buf.at[source(k), p, mine, :]
@@ -83,11 +89,45 @@
         piece = q_buf.at[source(k), :, mine, :]
         return remote(piece, piece, qs_send.at[k], qs_recv.at[k], sibling)
 
-    for p in range(PIECES):
-        q_in[p].wait()
-        q_copy(0, p, 0, 1, outer).start()
-        q_copy(0, p, 1, 2 + mid, second).start()
+    for copy in q_in:
+        copy.wait()
+
+    @pl.when(mid == 1)
+    def _():
+        for p in range(PIECES):
+            q_copy(0, p, 0, 1, outer).start()
+            q_copy(0, p, 1, 3, second).start()
+
+    @pl.when(mid == 0)
+    def _():
+        for p in range(PIECES):
+            q_copy(0, p, 0, 1, outer).start()
+        for p in range(PIECES):
+            q_copy(0, p, 1, 2, second).start()
+
     q_share(0).start()
+    inv_in.start()
+    docs_in.start()
+
+    @pl.when(c == 1)
+    def _():
+        greet(partner)
+
+        def greet_peer(i, _):
+            greet(peer(i))
+            return 0
+
+        lax.fori_loop(1, 16, greet_peer, 0)
+
+    def plane_ready():
+        @pl.when(c == 1)
+        def _():
+            pl.semaphore_wait(barrier, 16)
+            tell(plane_sem)
+
+        @pl.when(c == 0)
+        def _():
+            pl.semaphore_wait(plane_sem, 1)
 
     def place(s):
         return 1 - (s + s // 2) % 2, s // 2
@@ -114,55 +154,96 @@
         half, j = place(s)
         p_buf[half, z, c, pl.ds(pl.multiple_of(j * BATCH, BATCH), BATCH), :] = pre.astype(jnp.bfloat16)
 
+    def outward(k):
+        half, j = place(source(k))
+        p_copy(0, half, j, 0, 1, outer).start()
+
     def spread(k):
         half, j = place(source(k))
-        p_copy(0, half, j, 0, 1, outer).start()
         p_copy(0, half, j, 1, 2 + mid, second).start()
         p_share(0, half, j).start()
 
+    def q_relay(k, p):
+        q_copy(k, p, 0, k, outer).wait_recv()
+        q_copy(k, p, k, 5 - k, outer).start()
+
+    def p_relay(k, half):
+        for j in range(2):
+            p_copy(k, half, j, 0, k, outer).wait_recv()
+            p_copy(k, half, j, k, 5 - k, outer).start()
+            p_share(k, half, j).start()
+
     inv_in.wait()
-    precondition(0)
 
     @pl.when(mid == 1)
     def _():
-        def relay(p, _):
-            for k in (3, 2):
-                q_copy(k, p, 0, k, outer).wait_recv()
-                q_copy(k, p, k, 5 - k, outer).start()
+        precondition(0)
+        spread(0)
+        for p in range(PIECES):
+            q_relay(3, p)
+        q_share(3).start()
+        for p in range(PIECES):
+            q_copy(1, p, 0, 1, outer).wait_recv()
+        q_share(1).start()
+        q_relay(2, 0)
+        q_relay(2, 1)
+        precondition(3)
+        spread(3)
+        q_relay(2, 2)
+        q_relay(2, 3)
+        q_share(2).start()
+        outward(0)
+        outward(3)
+        precondition(1)
+        spread(1)
+        precondition(2)
+        spread(2)
+        p_relay(3, 0)
+        p_relay(2, 0)
+        outward(1)
+        outward(2)
+        p_relay(3, 1)
+        p_relay(2, 1)
+        for half in range(2):
+            for j in range(2):
+                p_copy(1, half, j, 0, 1, outer).wait_recv()
+                p_share(1, half, j).start()
+
+    @pl.when(mid == 0)
+    def _():
+        def batch(k, _):
+            @pl.when(k > 0)
+            def _():
+                for p in range(PIECES):
+                    q_copy(k, p, 0, k, outer).wait_recv()
+                q_share(k).start()
+
+            precondition(k)
+            outward(k)
+            spread(k)
             return 0
 
-        lax.fori_loop(0, PIECES, relay, 0)
-
-    spread(0)
-
-    def gather(step, _):
-        k = (step + 2 * mid) % 3 + 1
-
-        @pl.when((mid == 0) | (k == 1))
+        lax.fori_loop(0, 4, batch, 0)
+
+    docs_in.wait()
+
+    def arrive(half, k):
+        @pl.when(mid == 0)
         def _():
-            for p in range(PIECES):
-                q_copy(k, p, 0, k, outer).wait_recv()
-
-        q_share(k).start()
-        precondition(k)
-        spread(k)
-        return 0
-
-    lax.fori_loop(0, 3, gather, 0)
-
-    docs_in.wait()
-
-    def score(half, k):
+            for j in range(2):
+                p_copy(k, half, j, 0, k, outer).wait_recv()
+                p_share(k, half, j).start()
+
+    def shared(half, k):
         for j in range(2):
             p_share(k, half, j).wait_recv()
+
+    def score(half, k, core, rows):
         s = source(k)
-        part = 0.0
-        for core in range(2):
-            columns = pl.ds(pl.multiple_of(s * 2 * COLS + core * COLS, COLS), COLS)
-            part += lax.dot_general(
-                docs_buf[:, columns], p_buf[half, s, core], NT, preferred_element_type=jnp.float32
-            )
-        return part
+        columns = pl.ds(pl.multiple_of((s * 2 + core) * COLS, COLS), COLS)
+        return lax.dot_general(
+            docs_buf[rows, columns], p_buf[half, s, core], NT, preferred_element_type=jnp.float32
+        )
 
     def sum_copy(half, i):
         return remote(
@@ -184,43 +265,50 @@
         total[half] = lax.fori_loop(1, 16, add, own[half])
         last_copy(half).start()
 
+    everything = pl.ds(0, ROWS)
     for half in range(2):
-        acc[...] = score(half, 0)
-
-        def step(i, _, half=half):
-            k = jnp.where(mid == 1, 3 - i, 1 + i)
-            for j in range(2):
-                p_copy(k, half, j, 0, k, outer).wait_recv()
-
-                @pl.when((mid == 1) & (i < 2))
+        shared(half, 0)
+        acc[...] = score(half, 0, c, everything) + score(half, 0, 1 - c, everything)
+
+        def step(k, _, half=half):
+            arrive(half, k)
+            shared(half, k)
+            acc[...] += score(half, k, c, everything) + score(half, k, 1 - c, everything)
+            return 0
+
+        lax.fori_loop(1, 3, step, 0)
+        arrive(half, 3)
+        if half == 0:
+            plane_ready()
+        acc[...] += score(half, 3, c, everything)
+        shared(half, 3)
+
+        def finish(n, _, half=half):
+            line = (y + 2 + n) % 4
+            rows = pl.ds(pl.multiple_of(line * 4 * BLOCK, 4 * BLOCK), 4 * BLOCK)
+            done = acc[rows, :] + score(half, 3, 1 - c, rows)
+            acc[rows, :] = done
+            sbuf[half, pl.ds(line * 4, 4)] = done.astype(jnp.bfloat16).reshape(4, BLOCK, HALF)
+            for m in range(4):
+                i = (2 + n) % 4 * 4 + (2 + m) % 4
+
+                @pl.when(i > 0)
                 def _():
-                    p_copy(k, half, j, k, 5 - k, outer).start()
-
-                p_share(k, half, j).start()
-            acc[...] += score(half, k)
+                    sum_copy(half, i).start()
+
             return 0
 
-        if half == 0:
-            lax.fori_loop(0, 3, step, 0)
-        else:
-            lax.fori_loop(0, 2, step, 0)
-            collect(0)
-            lax.fori_loop(2, 3, step, 0)
-        for block in range(16):
-            sbuf[half, block] = acc[pl.ds(block * BLOCK, BLOCK), :].astype(jnp.bfloat16)
+        lax.fori_loop(0, 4, finish, 0)
         own[half] = acc[pl.ds(pl.multiple_of(plane * BLOCK, BLOCK), BLOCK), :]
 
-        def send(i, _, half=half):
-            sum_copy(half, i).start()
-            return 0
-
-        lax.fori_loop(1, 16, send, 0)
-
+    collect(0)
     collect(1)
+    kept = pl.ds(pl.multiple_of(h * 32, 32), 32)
+    ready = []
     for half in range(2):
         last_copy(half).wait_recv()
-        rows = pl.ds(pl.multiple_of(h * 32, 32), 32)
-        o_ref[:, pl.ds(half * HALF, HALF)] = total[half, rows, :] + zbuf[half]
+        ready.append(total[half, kept, :] + zbuf[half])
+    o_ref[...] = jnp.concatenate([ready[1][:, :BATCH], ready[0], ready[1][:, BATCH:]], axis=1)
 
     for p in range(PIECES):
         q_copy(0, p, 0, 1, outer).wait_send()
@@ -239,14 +327,14 @@
                 for j in range(2):
                     p_copy(k, half, j, k, 5 - k, outer).wait_send()
 
-    def shared(k, _):
+    def handed(k, _):
         q_share(k).wait_send()
         for half in range(2):
             for j in range(2):
                 p_share(k, half, j).wait_send()
         return 0
 
-    lax.fori_loop(0, 4, shared, 0)
+    lax.fori_loop(0, 4, handed, 0)
 
     def sent(i, _):
         sum_copy(0, i).wait_send()
@@ -263,7 +351,7 @@
     bf16, f32 = jnp.bfloat16, jnp.float32
     out = pl.pallas_call(
         kernel,
-        out_shape=jax.ShapeDtypeStruct((32, Q), f32),
+        out_shape=pltpu.VMEM((32, Q), f32),
         in_specs=[pl.BlockSpec(memory_space=pl.ANY)] * 3,
         out_specs=pl.BlockSpec(memory_space=pltpu.VMEM),
         scratch_shapes=[
@@ -290,6 +378,8 @@
             dma((2, 15)),
             dma((2,)),
             dma((2,)),
+            pltpu.SemaphoreType.REGULAR,
+            pltpu.SemaphoreType.REGULAR,
         ],
         compiler_params=pltpu.CompilerParams(
             collective_id=0, has_side_effects=True, vmem_limit_bytes=60 * 2**20
@@ -297,7 +387,7 @@
         name="scores",
     )(query_grads[0], doc_grads[0], inverse[0])
     factor = 1.0 / math.sqrt(F * LAYERS)
-    return jnp.concatenate([out[:, 128:192], out[:, :128], out[:, 192:]], axis=1) * factor
+    return out * factor
 
 
 def solution(mesh):

time: 65 us -> 59.4 us (0.914)
  Pallas kernels: 62.5 us -> 58.7 us
  local copies, waits for them, and re-layouts: 1.59 us -> 0 us
    pallas_call x1, Pallas kernels: 62.5 us -> 58.7 us  [per_device(): pl.pallas_call(kernel, out_shape=pltpu.VMEM((32, Q), f32), in_specs=[pl.B...]
    slice x2 -> x0, local copies, waits for them, and re-layouts: 1.59 us -> none  [the longest x1 0.87 us: per_device(): out[:, 128:192]]
where the time goes in v2:
time: 59.4 us; the launch traced here: 59.3 us
  Pallas kernels  58.7 us (99%)
  other arithmetic  0.62 us (1%)
    pallas_call x1, Pallas kernels, per_device(): pl.pallas_call(kernel, out_shape=pltpu.VMEM((32, Q), f32), in_specs=[pl.B...  58.7 us

profile of v2, /device:TPU:1, one launch (start us, length us, event | category | flops | bytes accessed | tf_op | source)
XLA Modules:
  0.0 59.3 jit_solution(3866629331181554179)
XLA Ops:
  0.0 58.7 %scores.1 = f32[32,256]{1,0:T(8,128)S(1)} custom-call(bf16[32,4096]{1,0:T(8,128)(2,1)} %bitcast.5, bf16[1024,4096]{1,0:T(8,128)(2,1)} %bitcast.3, bf16[4096,512]{1,0:T(8,128)(2,1)} %bitcast.4), custom_call_target="tpu_custom_call" | custom-call | tf_op jit(solution)/shard_map/scores/pallas_call | solution.py:352
  58.7 0.6 %broadcast_multiply_fusion = f32[32,256]{1,0:T(8,128)} fusion(f32[32,256]{1,0:T(8,128)S(1)} %scores.1), kind=kLoop, calls=%fused_computation | loop fusion | flops 8192 | bytes 65536 | tf_op jit(solution)/shard_map/mul | solution.py:390

commit v3 on v2

v3 whole, which is shorter than its diff:
```python
import math

import jax
import jax.numpy as jnp
from jax import lax
from jax.experimental import pallas as pl
from jax.experimental.pallas import tpu as pltpu
from jax.sharding import PartitionSpec as P

F = 4096
LAYERS = 32
Q = 256
ROWS = 1024
BATCH = 64
HALF = 128
COLS = 512
PIECES = 4
WIDE = F // PIECES
BLOCK = 64
MESH = pl.DeviceIdType.MESH
NT = (((1,), (1,)), ((), ()))


def kernel(
    q_hbm, docs_hbm, inv_hbm, o_ref,
    q_buf, inv_buf, docs_buf, p_buf, acc, outbox, a_in, a_own, a_total, a_last,
    in_sem, q_send, q_recv, qs_send, qs_recv, p_send, p_recv, ps_send, ps_recv,
    a_send, a_recv, z_send, z_recv, line_sem, plane_sem,
):
    d, l = lax.axis_index("doc"), lax.axis_index("layer")
    z, c = d // 2, d % 2
    y, x, h = l // 8, (l // 2) % 4, l % 2
    plane = y * 4 + x
    mid = ((z + 1) // 2) % 2
    outer = z + 1 - 2 * (z % 2)
    second = 2 - z // 2
    partner = (d, l + 1 - 2 * h)
    sibling = (z * 2 + 1 - c, l)

    def peer(i):
        return (d, ((y + i // 4) % 4) * 8 + ((x + i % 4) % 4) * 2 + h)

    def source(k):
        return jnp.where(k == 0, z, jnp.where(k == 1, outer, jnp.where(k == 2, (z + 2) % 4, 3 - z)))

    def remote(src, dst, ss, rs, to):
        return pltpu.make_async_remote_copy(
            src_ref=src, dst_ref=dst, send_sem=ss, recv_sem=rs, device_id=to, device_id_type=MESH
        )

    mine = pl.ds(pl.multiple_of(c * 32, 32), 32)
    q_in = [
        pltpu.make_async_copy(
            q_hbm.at[:, pl.ds(p * WIDE, WIDE)], q_buf.at[z, p, mine, :], in_sem.at[p]
        )
        for p in range(PIECES)
    ]
    inv_in = pltpu.make_async_copy(inv_hbm, inv_buf, in_sem.at[PIECES])
    docs_in = pltpu.make_async_copy(docs_hbm, docs_buf, in_sem.at[PIECES + 1])
    for copy in q_in:
        copy.start()

    barrier = pltpu.get_barrier_semaphore()

    def greet(to):
        pl.semaphore_signal(barrier, inc=1, device_id=to, device_id_type=MESH)

    def tell(semaphore):
        pl.semaphore_signal(semaphore, inc=1, device_id=sibling, device_id_type=MESH)

    @pl.when(c == 0)
    def _():
        greet((outer * 2, l))

        @pl.when(mid == 1)
        def _():
            greet((second * 2, l))

        pl.semaphore_wait(barrier, 3 + 2 * mid)
        tell(line_sem)

    @pl.when(c == 1)
    def _():
        greet(sibling)
        greet((outer * 2, l))

        @pl.when(mid == 1)
        def _():
            greet((second * 2, l))

        pl.semaphore_wait(line_sem, 1)

    def q_copy(k, p, slot, at_k, to):
        piece = q_buf.at[source(k), p, mine, :]
        return remote(piece, piece, q_send.at[slot, p], q_recv.at[at_k - 1, p], (to * 2 + c, l))

    def q_share(k):
        piece = q_buf.at[source(k), :, mine, :]
        return remote(piece, piece, qs_send.at[k], qs_recv.at[k], sibling)

    for copy in q_in:
        copy.wait()

    def depart(p, _):
        q_copy(0, p, 0, 1, outer).start()

        @pl.when(mid == 1)
        def _():
            q_copy(0, p, 1, 3, second).start()

        return 0

    lax.fori_loop(0, PIECES, depart, 0)
    q_share(0).start()
    inv_in.start()
    docs_in.start()

    @pl.when(c == 1)
    def _():
        greet(partner)

        def greet_peer(i, _):
            greet(peer(i))
            return 0

        lax.fori_loop(1, 16, greet_peer, 0)

    def plane_ready():
        @pl.when(c == 1)
        def _():
            pl.semaphore_wait(barrier, 16)
            tell(plane_sem)

        @pl.when(c == 0)
        def _():
            pl.semaphore_wait(plane_sem, 1)

    def place(s):
        return 1 - (s + s // 2) % 2, s // 2

    def p_ref(half, s, core, j):
        return p_buf.at[half, s, core, pl.ds(pl.multiple_of(j * BATCH, BATCH), BATCH), :]

    def p_copy(k, half, j, slot, at_k, to):
        piece = p_ref(half, source(k), c, j)
        return remote(piece, piece, p_send.at[slot, half, j], p_recv.at[at_k - 1, half, j], (to * 2 + c, l))

    def p_share(k, half, j):
        piece = p_ref(half, source(k), c, j)
        return remote(piece, piece, ps_send.at[k, half, j], ps_recv.at[k, half, j], sibling)

    def precondition(k):
        q_share(k).wait_recv()
        s = source(k)
        pre = jnp.dot(q_buf[s, 0], inv_buf[pl.ds(0, WIDE), :], preferred_element_type=jnp.float32)
        for p in range(1, PIECES):
            pre += jnp.dot(
                q_buf[s, p], inv_buf[pl.ds(p * WIDE, WIDE), :], preferred_element_type=jnp.float32
            )
        half, j = place(s)
        p_buf[half, z, c, pl.ds(pl.multiple_of(j * BATCH, BATCH), BATCH), :] = pre.astype(jnp.bfloat16)

    def outward(k):
        half, j = place(source(k))
        p_copy(0, half, j, 0, 1, outer).start()

    def spread(k):
        half, j = place(source(k))
        p_share(0, half, j).start()

        @pl.when(mid == 1)
        def _():
            p_copy(0, half, j, 1, 3, second).start()

    def q_relay(k, p):
        q_copy(k, p, 0, k, outer).wait_recv()
        if k == 1:
            q_copy(1, p, 4, 2, second).start()
        else:
            q_copy(k, p, k, 5 - k, outer).start()

    def p_relay(k, half, j):
        p_copy(k, half, j, 0, k, outer).wait_recv()
        if k == 1:
            p_copy(1, half, j, 4, 2, second).start()
        else:
            p_copy(k, half, j, k, 5 - k, outer).start()
        p_share(k, half, j).start()

    def q_arrive(k):
        def step(p, _):
            q_copy(k, p, 0, k, outer).wait_recv()
            return 0

        lax.fori_loop(0, PIECES, step, 0)

    def q_relays(ks, first, last):
        def step(p, _):
            for k in ks:
                q_relay(k, p)
            return 0

        lax.fori_loop(first, last, step, 0)

    inv_in.wait()
    early = z // 2

    def batch(n, _):
        k = jnp.where((mid == 0) | (n == 0), n, (n + 1) % 3 + 1)

        @pl.when((mid == 0) & (n > 0))
        def _():
            q_arrive(k)
            q_share(k).start()

        precondition(k)
        spread(k)

        @pl.when(mid == 0)
        def _():
            outward(k)

        @pl.when((mid == 1) & (n == 0))
        def _():
            q_relays((3, 1), 0, PIECES)
            q_share(3).start()
            q_share(1).start()
            q_relays((2,), 0, PIECES // 2)

        @pl.when((mid == 1) & (n == 1))
        def _():
            q_relays((2,), PIECES // 2, PIECES)
            q_share(2).start()
            outward(0)
            outward(3)
            p_relay(1, 1, early)
            p_relay(1, 0, early)

        return 0

    lax.fori_loop(0, 4, batch, 0)

    @pl.when(mid == 1)
    def _():
        p_relay(3, 0, 0)
        p_relay(3, 0, 1)
        outward(1)
        outward(2)
        p_relay(2, 0, 1 - early)
        p_relay(1, 0, 1 - early)
        p_relay(2, 0, early)
        p_relay(3, 1, 0)
        p_relay(3, 1, 1)
        p_relay(2, 1, 1 - early)

    docs_in.wait()

    def a_copy(half, i):
        to = ((y + i // 4) % 4) * 4 + (x + i % 4) % 4
        return remote(
            outbox.at[half, pl.ds(to * 2, 2)], a_in.at[half, i - 1],
            a_send.at[half, i - 1], a_recv.at[half, i - 1], peer(i),
        )

    def a_partner(half):
        return remote(a_total.at[half, 1 - h], a_last.at[half], z_send.at[half], z_recv.at[half], partner)

    def distance(n):
        return jnp.where(n < 2, 2 + n, 3 - n)

    def score(half, s, core):
        columns = pl.ds(pl.multiple_of((s * 2 + core) * COLS, COLS), COLS)
        return lax.dot_general(
            docs_buf[:, columns], p_buf[half, s, core], NT, preferred_element_type=jnp.float32
        )

    def shared(half, k):
        for j in range(2):
            p_share(k, half, j).wait_recv()

    def hand_out(half):
        def step(n, _):
            line = (y + distance(n)) % 4
            rows = pl.ds(pl.multiple_of(line * 4 * BLOCK, 4 * BLOCK), 4 * BLOCK)
            outbox[half, pl.ds(line * 8, 8)] = acc[rows, :].astype(jnp.bfloat16).reshape(8, 32, HALF)

            def send(m, _):
                i = distance(n) * 4 + distance(m)

                @pl.when(i > 0)
                def _():
                    a_copy(half, i).start()

                return 0

            for m in range(4):
                send(m, 0)
            return 0

        lax.fori_loop(0, 4, step, 0)

    def source_step(n, _):
        half, k = n // 4, n % 4

        @pl.when((mid == 0) & (k > 0))
        def _():
            for j in range(2):
                p_copy(k, half, j, 0, k, outer).wait_recv()
                p_share(k, half, j).start()

        @pl.when((mid == 1) & (n == 4))
        def _():
            p_relay(1, 1, 1 - early)
            p_relay(2, 1, early)

        @pl.when(n == 3)
        def _():
            plane_ready()

        s = source(k)

        @pl.when(k < 3)
        def _():
            shared(half, k)
            before = jnp.where(k == 0, 0.0, acc[...])
            acc[...] = before + (score(half, s, 0) + score(half, s, 1))

        @pl.when(k == 3)
        def _():
            def turn(t, _):
                @pl.when(t == 1)
                def _():
                    shared(half, k)

                acc[...] += score(half, s, (c + t) % 2)
                return 0

            lax.fori_loop(0, 2, turn, 0)
            hand_out(half)

        @pl.when(k == 3)
        def _():
            a_own[half] = acc[pl.ds(pl.multiple_of(plane * BLOCK, BLOCK), BLOCK), :].reshape(2, 32, HALF)

        return 0

    lax.fori_loop(0, 8, source_step, 0)

    def collect(half):
        def add(i, running):
            a_copy(half, i).wait()
            return running + a_in[half, i - 1, 1 - h].astype(jnp.float32)

        a_total[half, 1 - h] = lax.fori_loop(1, 16, add, a_own[half, 1 - h], unroll=True)
        a_partner(half).start()

        def keep(i, running):
            return running + a_in[half, i - 1, h].astype(jnp.float32)

        a_total[half, h] = lax.fori_loop(1, 16, keep, a_own[half, h], unroll=True)

    collect(0)
    def q_left(p, _):
        q_copy(0, p, 0, 1, outer).wait_send()

        @pl.when(mid == 1)
        def _():
            q_copy(0, p, 1, 3, second).wait_send()
            q_copy(1, p, 4, 2, second).wait_send()
            q_copy(3, p, 3, 2, outer).wait_send()
            q_copy(2, p, 2, 3, outer).wait_send()

        q_share(p).wait_send()
        return 0

    lax.fori_loop(0, PIECES, q_left, 0)

    def p_left(n, _):
        half, j = n // 2, n % 2
        p_copy(0, half, j, 0, 1, outer).wait_send()

        @pl.when(mid == 1)
        def _():
            p_copy(0, half, j, 1, 3, second).wait_send()
            p_copy(1, half, j, 4, 2, second).wait_send()
            p_copy(3, half, j, 3, 2, outer).wait_send()
            p_copy(2, half, j, 2, 3, outer).wait_send()

        for k in range(4):
            p_share(k, half, j).wait_send()
        return 0

    lax.fori_loop(0, 4, p_left, 0)

    collect(1)
    a_partner(0).wait()
    a_done = a_total[0, h] + a_last[0]
    a_partner(1).wait()
    b_done = a_total[1, h] + a_last[1]
    o_ref[...] = jnp.concatenate([b_done[:, :BATCH], a_done, b_done[:, BATCH:]], axis=1)


def per_device(query_grads, doc_grads, inverse):
    dma = pltpu.SemaphoreType.DMA
    bf16, f32 = jnp.bfloat16, jnp.float32
    out = pl.pallas_call(
        kernel,
        out_shape=pltpu.VMEM((32, Q), f32),
        in_specs=[pl.BlockSpec(memory_space=pl.ANY)] * 3,
        out_specs=pl.BlockSpec(memory_space=pltpu.VMEM),
        scratch_shapes=[
            pltpu.VMEM((4, PIECES, BATCH, WIDE), bf16),
            pltpu.VMEM((F, COLS), bf16),
            pltpu.VMEM((ROWS, F), bf16),
            pltpu.VMEM((2, 4, 2, HALF, COLS), bf16),
            pltpu.VMEM((ROWS, HALF), f32),
            pltpu.VMEM((2, 32, 32, HALF), bf16),
            pltpu.VMEM((2, 15, 2, 32, HALF), bf16),
            pltpu.VMEM((2, 2, 32, HALF), f32),
            pltpu.VMEM((2, 2, 32, HALF), f32),
            pltpu.VMEM((2, 32, HALF), f32),
            dma((PIECES + 2,)),
            dma((5, PIECES)),
            dma((3, PIECES)),
            dma((4,)),
            dma((4,)),
            dma((5, 2, 2)),
            dma((3, 2, 2)),
            dma((4, 2, 2)),
            dma((4, 2, 2)),
            dma((2, 15)),
            dma((2, 15)),
            dma((2,)),
            dma((2,)),
            pltpu.SemaphoreType.REGULAR,
            pltpu.SemaphoreType.REGULAR,
        ],
        compiler_params=pltpu.CompilerParams(
            collective_id=0, has_side_effects=True, vmem_limit_bytes=60 * 2**20
        ),
        name="scores",
    )(query_grads[0], doc_grads[0], inverse[0])
    factor = 1.0 / math.sqrt(F * LAYERS)
    return out * factor


def solution(mesh):
    in_specs = (P("layer", "doc", None), P("layer", "doc", None), P("layer", None, "doc"))
    out_specs = P(("doc", "layer"), None)
    return jax.shard_map(
        per_device, mesh=mesh, in_specs=in_specs, out_specs=out_specs, check_vma=False
    )
```

time: 59.4 us -> 58.5 us (0.985)
  Pallas kernels: 58.7 us -> 57.3 us
    pallas_call x1, Pallas kernels: 58.7 us -> 57.3 us  [per_device(): pl.pallas_call(kernel, out_shape=pltpu.VMEM((32, Q), f32), in_specs=[pl.B...]
where the time goes in v3:
time: 58.5 us; the launch traced here: 57.9 us
  Pallas kernels  57.3 us (98%)
  other arithmetic  0.62 us (1%)
    pallas_call x1, Pallas kernels, per_device(): pl.pallas_call(kernel, out_shape=pltpu.VMEM((32, Q), f32), in_specs=[pl.B...  57.3 us

profile of v3, /device:TPU:1, one launch (start us, length us, event | category | flops | bytes accessed | tf_op | source)
XLA Modules:
  0.0 57.9 jit_solution(1924700438176628758)
XLA Ops:
  0.0 57.3 %scores.1 = f32[32,256]{1,0:T(8,128)S(1)} custom-call(bf16[32,4096]{1,0:T(8,128)(2,1)} %bitcast.5, bf16[1024,4096]{1,0:T(8,128)(2,1)} %bitcast.3, bf16[4096,512]{1,0:T(8,128)(2,1)} %bitcast.4), custom_call_target="tpu_custom_call" | custom-call | tf_op jit(solution)/shard_map/scores/pallas_call | solution.py:406
  57.3 0.6 %broadcast_multiply_fusion = f32[32,256]{1,0:T(8,128)} fusion(f32[32,256]{1,0:T(8,128)S(1)} %scores.1), kind=kLoop, calls=%fused_computation | loop fusion | flops 8192 | bytes 65536 | tf_op jit(solution)/shard_map/mul | solution.py:444

commit v4 on v3

--- a/solution.py
+++ b/solution.py
@@ -23,9 +23,9 @@
 
 def kernel(
     q_hbm, docs_hbm, inv_hbm, o_ref,
-    q_buf, inv_buf, docs_buf, p_buf, acc, outbox, a_in, a_own, a_total, a_last,
+    q_buf, inv_buf, docs_buf, p_buf, acc, outbox, a_in, a_own, a_total, a_last, c_in,
     in_sem, q_send, q_recv, qs_send, qs_recv, p_send, p_recv, ps_send, ps_recv,
-    a_send, a_recv, z_send, z_recv, line_sem, plane_sem,
+    a_send, a_recv, c_send, c_recv, z_send, z_recv, line_sem, plane_sem,
 ):
     d, l = lax.axis_index("doc"), lax.axis_index("layer")
     z, c = d // 2, d % 2
@@ -39,6 +39,9 @@
 
     def peer(i):
         return (d, ((y + i // 4) % 4) * 8 + ((x + i % 4) % 4) * 2 + h)
+
+    def owner(i):
+        return ((y + i // 8) % 4) * 8 + ((x + i // 2 % 4) % 4) * 2 + (h + i % 2) % 2
 
     def source(k):
         return jnp.where(k == 0, z, jnp.where(k == 1, outer, jnp.where(k == 2, (z + 2) % 4, 3 - z)))
@@ -117,18 +120,16 @@
 
     @pl.when(c == 1)
     def _():
-        greet(partner)
-
-        def greet_peer(i, _):
-            greet(peer(i))
+        def greet_owner(i, _):
+            greet((d, owner(i)))
             return 0
 
-        lax.fori_loop(1, 16, greet_peer, 0)
+        lax.fori_loop(1, 32, greet_owner, 0)
 
     def plane_ready():
         @pl.when(c == 1)
         def _():
-            pl.semaphore_wait(barrier, 16)
+            pl.semaphore_wait(barrier, 31)
             tell(plane_sem)
 
         @pl.when(c == 0)
@@ -244,11 +245,11 @@
     def _():
         p_relay(3, 0, 0)
         p_relay(3, 0, 1)
+        p_relay(2, 0, 1 - early)
         outward(1)
-        outward(2)
-        p_relay(2, 0, 1 - early)
         p_relay(1, 0, 1 - early)
         p_relay(2, 0, early)
+        outward(2)
         p_relay(3, 1, 0)
         p_relay(3, 1, 1)
         p_relay(2, 1, 1 - early)
@@ -262,6 +263,17 @@
             a_send.at[half, i - 1], a_recv.at[half, i - 1], peer(i),
         )
 
+    def b_copy(i):
+        to = ((y + i // 4) % 4) * 4 + (x + i % 4) % 4
+        return remote(
+            outbox.at[1, to * 2 + 1], a_in.at[1, i - 1, 1],
+            a_send.at[1, i - 1], a_recv.at[1, i - 1], peer(i),
+        )
+
+    def c_copy(i):
+        to = (((y + i // 4) % 4) * 4 + (x + i % 4) % 4) * 2 + 1 - h
+        return remote(outbox.at[1, to], c_in.at[i], c_send.at[i], c_recv.at[i], (d, to))
+
     def a_partner(half):
         return remote(a_total.at[half, 1 - h], a_last.at[half], z_send.at[half], z_recv.at[half], partner)
 
@@ -284,17 +296,21 @@
             rows = pl.ds(pl.multiple_of(line * 4 * BLOCK, 4 * BLOCK), 4 * BLOCK)
             outbox[half, pl.ds(line * 8, 8)] = acc[rows, :].astype(jnp.bfloat16).reshape(8, 32, HALF)
 
-            def send(m, _):
-                i = distance(n) * 4 + distance(m)
-
-                @pl.when(i > 0)
+            for m in range(4):
+                i = distance(n) * 4 + (2, 3, 1, 0)[m]
+
+                @pl.when((half == 1) & (h == 1))
+                def _():
+                    c_copy(i).start()
+
+                    @pl.when(i > 0)
+                    def _():
+                        b_copy(i).start()
+
+                @pl.when(((half == 0) | (h == 0)) & (i > 0))
                 def _():
                     a_copy(half, i).start()
 
-                return 0
-
-            for m in range(4):
-                send(m, 0)
             return 0
 
         lax.fori_loop(0, 4, step, 0)
@@ -392,11 +408,33 @@
 
     lax.fori_loop(0, 4, p_left, 0)
 
-    collect(1)
+
+    @pl.when(h == 0)
+    def _():
+        collect(1)
+
+        def cross(i, running):
+            c_copy(i).wait_recv()
+            return running + c_in[i].astype(jnp.float32)
+
+        a_total[1, 0] = lax.fori_loop(0, 16, cross, a_total[1, 0], unroll=True)
+        a_partner(1).wait_send()
+
+    @pl.when(h == 1)
+    def _():
+        def add(i, running):
+            b_copy(i).wait()
+            return running + a_in[1, i - 1, 1].astype(jnp.float32)
+
+        kept = lax.fori_loop(1, 16, add, a_own[1, 1], unroll=True)
+        for i in range(16):
+            c_copy(i).wait_send()
+        a_partner(1).wait_recv()
+        a_total[1, 1] = kept + a_last[1]
+
     a_partner(0).wait()
     a_done = a_total[0, h] + a_last[0]
-    a_partner(1).wait()
-    b_done = a_total[1, h] + a_last[1]
+    b_done = a_total[1, h]
     o_ref[...] = jnp.concatenate([b_done[:, :BATCH], a_done, b_done[:, BATCH:]], axis=1)
 
 
@@ -419,6 +457,7 @@
             pltpu.VMEM((2, 2, 32, HALF), f32),
             pltpu.VMEM((2, 2, 32, HALF), f32),
             pltpu.VMEM((2, 32, HALF), f32),
+            pltpu.VMEM((16, 32, HALF), bf16),
             dma((PIECES + 2,)),
             dma((5, PIECES)),
             dma((3, PIECES)),
@@ -430,6 +469,8 @@
             dma((4, 2, 2)),
             dma((2, 15)),
             dma((2, 15)),
+            dma((16,)),
+            dma((16,)),
             dma((2,)),
             dma((2,)),
             pltpu.SemaphoreType.REGULAR,

time: 58.5 us -> 57 us (0.974)
  Pallas kernels: 57.3 us -> 56.3 us
    pallas_call x1, Pallas kernels: 57.3 us -> 56.3 us  [per_device(): pl.pallas_call(kernel, out_shape=pltpu.VMEM((32, Q), f32), in_specs=[pl.B...]
where the time goes in v4:
time: 57 us; the launch traced here: 56.9 us
  Pallas kernels  56.3 us (99%)
  other arithmetic  0.62 us (1%)
    pallas_call x1, Pallas kernels, per_device(): pl.pallas_call(kernel, out_shape=pltpu.VMEM((32, Q), f32), in_specs=[pl.B...  56.3 us

profile of v4, /device:TPU:1, one launch (start us, length us, event | category | flops | bytes accessed | tf_op | source)
XLA Modules:
  0.0 56.9 jit_solution(16094958024817852616)
XLA Ops:
  0.0 56.3 %scores.1 = f32[32,256]{1,0:T(8,128)S(1)} custom-call(bf16[32,4096]{1,0:T(8,128)(2,1)} %bitcast.5, bf16[1024,4096]{1,0:T(8,128)(2,1)} %bitcast.3, bf16[4096,512]{1,0:T(8,128)(2,1)} %bitcast.4), custom_call_target="tpu_custom_call" | custom-call | tf_op jit(solution)/shard_map/scores/pallas_call | solution.py:444
  56.3 0.6 %broadcast_multiply_fusion = f32[32,256]{1,0:T(8,128)} fusion(f32[32,256]{1,0:T(8,128)S(1)} %scores.1), kind=kLoop, calls=%fused_computation | loop fusion | flops 8192 | bytes 65536 | tf_op jit(solution)/shard_map/mul | solution.py:485

commit v5 on v4

--- a/solution.py
+++ b/solution.py
@@ -71,25 +71,25 @@
     def tell(semaphore):
         pl.semaphore_signal(semaphore, inc=1, device_id=sibling, device_id_type=MESH)
 
-    @pl.when(c == 0)
-    def _():
-        greet((outer * 2, l))
-
-        @pl.when(mid == 1)
-        def _():
-            greet((second * 2, l))
+    @pl.when(c == 1)
+    def _():
+        greet((outer * 2 + 1, l))
+
+        @pl.when(mid == 1)
+        def _():
+            greet((second * 2 + 1, l))
 
         pl.semaphore_wait(barrier, 3 + 2 * mid)
         tell(line_sem)
 
-    @pl.when(c == 1)
+    @pl.when(c == 0)
     def _():
         greet(sibling)
-        greet((outer * 2, l))
-
-        @pl.when(mid == 1)
-        def _():
-            greet((second * 2, l))
+        greet((outer * 2 + 1, l))
+
+        @pl.when(mid == 1)
+        def _():
+            greet((second * 2 + 1, l))
 
         pl.semaphore_wait(line_sem, 1)
 
@@ -118,7 +118,7 @@
     inv_in.start()
     docs_in.start()
 
-    @pl.when(c == 1)
+    @pl.when(c == 0)
     def _():
         def greet_owner(i, _):
             greet((d, owner(i)))
@@ -127,12 +127,12 @@
         lax.fori_loop(1, 32, greet_owner, 0)
 
     def plane_ready():
-        @pl.when(c == 1)
+        @pl.when(c == 0)
         def _():
             pl.semaphore_wait(barrier, 31)
             tell(plane_sem)
 
-        @pl.when(c == 0)
+        @pl.when(c == 1)
         def _():
             pl.semaphore_wait(plane_sem, 1)
 
@@ -280,10 +280,10 @@
     def distance(n):
         return jnp.where(n < 2, 2 + n, 3 - n)
 
-    def score(half, s, core):
+    def score(half, s, core, rows=pl.ds(0, ROWS)):
         columns = pl.ds(pl.multiple_of((s * 2 + core) * COLS, COLS), COLS)
         return lax.dot_general(
-            docs_buf[:, columns], p_buf[half, s, core], NT, preferred_element_type=jnp.float32
+            docs_buf[rows, columns], p_buf[half, s, core], NT, preferred_element_type=jnp.float32
         )
 
     def shared(half, k):
@@ -294,7 +294,13 @@
         def step(n, _):
             line = (y + distance(n)) % 4
             rows = pl.ds(pl.multiple_of(line * 4 * BLOCK, 4 * BLOCK), 4 * BLOCK)
-            outbox[half, pl.ds(line * 8, 8)] = acc[rows, :].astype(jnp.bfloat16).reshape(8, 32, HALF)
+            done = acc[rows, :] + score(half, source(3), 1 - c, rows)
+            outbox[half, pl.ds(line * 8, 8)] = done.astype(jnp.bfloat16).reshape(8, 32, HALF)
+
+            @pl.when(n == 3)
+            def _():
+                acc[rows, :] = done
+
 
             for m in range(4):
                 i = distance(n) * 4 + (2, 3, 1, 0)[m]
@@ -343,15 +349,8 @@
 
         @pl.when(k == 3)
         def _():
-            def turn(t, _):
-                @pl.when(t == 1)
-                def _():
-                    shared(half, k)
-
-                acc[...] += score(half, s, (c + t) % 2)
-                return 0
-
-            lax.fori_loop(0, 2, turn, 0)
+            acc[...] += score(half, s, c)
+            shared(half, k)
             hand_out(half)
 
         @pl.when(k == 3)

time: 57 us -> 56.2 us (0.986)
  Pallas kernels: 56.3 us -> 55.4 us
    pallas_call x1, Pallas kernels: 56.3 us -> 55.4 us  [per_device(): pl.pallas_call(kernel, out_shape=pltpu.VMEM((32, Q), f32), in_specs=[pl.B...]
where the time goes in v5:
time: 56.2 us; the launch traced here: 56 us
  Pallas kernels  55.4 us (99%)
  other arithmetic  0.62 us (1%)
    pallas_call x1, Pallas kernels, per_device(): pl.pallas_call(kernel, out_shape=pltpu.VMEM((32, Q), f32), in_specs=[pl.B...  55.4 us

profile of v5, /device:TPU:1, one launch (start us, length us, event | category | flops | bytes accessed | tf_op | source)
XLA Modules:
  0.0 56.0 jit_solution(1403378848578798955)
XLA Ops:
  0.0 55.4 %scores.1 = f32[32,256]{1,0:T(8,128)S(1)} custom-call(bf16[32,4096]{1,0:T(8,128)(2,1)} %bitcast.5, bf16[1024,4096]{1,0:T(8,128)(2,1)} %bitcast.3, bf16[4096,512]{1,0:T(8,128)(2,1)} %bitcast.4), custom_call_target="tpu_custom_call" | custom-call | tf_op jit(solution)/shard_map/scores/pallas_call | solution.py:443
  55.4 0.6 %broadcast_multiply_fusion = f32[32,256]{1,0:T(8,128)} fusion(f32[32,256]{1,0:T(8,128)S(1)} %scores.1), kind=kLoop, calls=%fused_computation | loop fusion | flops 8192 | bytes 65536 | tf_op jit(solution)/shard_map/mul | solution.py:484

commit v6 on v5

--- a/solution.py
+++ b/solution.py
@@ -292,34 +292,46 @@
 
     def hand_out(half):
         def step(n, _):
-            line = (y + distance(n)) % 4
+            line, away = n, (n + 4 - y) % 4
             rows = pl.ds(pl.multiple_of(line * 4 * BLOCK, 4 * BLOCK), 4 * BLOCK)
             done = acc[rows, :] + score(half, source(3), 1 - c, rows)
             outbox[half, pl.ds(line * 8, 8)] = done.astype(jnp.bfloat16).reshape(8, 32, HALF)
 
-            @pl.when(n == 3)
+            @pl.when(line == y)
             def _():
                 acc[rows, :] = done
 
-
-            for m in range(4):
-                i = distance(n) * 4 + (2, 3, 1, 0)[m]
-
-                @pl.when((half == 1) & (h == 1))
-                def _():
-                    c_copy(i).start()
+            @pl.when((half == 1) & (h == 1))
+            def _():
+                for m in (2, 3, 1, 0):
+                    c_copy(away * 4 + m).start()
+
+            @pl.when((half == 0) | (h == 0))
+            def _():
+                for m in (2, 3, 1, 0):
+                    i = away * 4 + m
+
+                    @pl.when(i > 0)
+                    def _():
+                        a_copy(half, i).start()
+
+            return 0
+
+        lax.fori_loop(0, 4, step, 0)
+
+        @pl.when((half == 1) & (h == 1))
+        def _():
+            def rest(n, _):
+                for m in (2, 3, 1, 0):
+                    i = distance(n) * 4 + m
 
                     @pl.when(i > 0)
                     def _():
                         b_copy(i).start()
 
-                @pl.when(((half == 0) | (h == 0)) & (i > 0))
-                def _():
-                    a_copy(half, i).start()
-
-            return 0
-
-        lax.fori_loop(0, 4, step, 0)
+                return 0
+
+            lax.fori_loop(0, 4, rest, 0)
 
     def source_step(n, _):
         half, k = n // 4, n % 4

time: 56.2 us -> 55.2 us (0.982)
  Pallas kernels: 55.4 us -> 54.4 us
    pallas_call x1, Pallas kernels: 55.4 us -> 54.4 us  [per_device(): pl.pallas_call(kernel, out_shape=pltpu.VMEM((32, Q), f32), in_specs=[pl.B...]
where the time goes in v6:
time: 55.2 us; the launch traced here: 55 us
  Pallas kernels  54.4 us (99%)
  other arithmetic  0.62 us (1%)
    pallas_call x1, Pallas kernels, per_device(): pl.pallas_call(kernel, out_shape=pltpu.VMEM((32, Q), f32), in_specs=[pl.B...  54.4 us

profile of v6, /device:TPU:1, one launch (start us, length us, event | category | flops | bytes accessed | tf_op | source)
XLA Modules:
  0.0 55.0 jit_solution(6716359927053630523)
XLA Ops:
  0.0 54.4 %scores.1 = f32[32,256]{1,0:T(8,128)S(1)} custom-call(bf16[32,4096]{1,0:T(8,128)(2,1)} %bitcast.5, bf16[1024,4096]{1,0:T(8,128)(2,1)} %bitcast.3, bf16[4096,512]{1,0:T(8,128)(2,1)} %bitcast.4), custom_call_target="tpu_custom_call" | custom-call | tf_op jit(solution)/shard_map/scores/pallas_call | solution.py:455
  54.4 0.6 %broadcast_multiply_fusion = f32[32,256]{1,0:T(8,128)} fusion(f32[32,256]{1,0:T(8,128)S(1)} %scores.1), kind=kLoop, calls=%fused_computation | loop fusion | flops 8192 | bytes 65536 | tf_op jit(solution)/shard_map/mul | solution.py:496

commit v7 on v6

--- a/solution.py
+++ b/solution.py
@@ -338,7 +338,8 @@
 
         @pl.when((mid == 0) & (k > 0))
         def _():
-            for j in range(2):
+            for turn in range(2):
+                j = (turn + 1 + early) % 2
                 p_copy(k, half, j, 0, k, outer).wait_recv()
                 p_share(k, half, j).start()
 
@@ -423,13 +424,14 @@
     @pl.when(h == 0)
     def _():
         collect(1)
-
-        def cross(i, running):
+        a_partner(0).wait()
+
+        a_partner(1).wait_send()
+        running = a_total[1, 0]
+        for i in (0, 1, 3, 4, 12, 2, 5, 7, 8, 13, 15, 6, 9, 11, 14, 10):
             c_copy(i).wait_recv()
-            return running + c_in[i].astype(jnp.float32)
-
-        a_total[1, 0] = lax.fori_loop(0, 16, cross, a_total[1, 0], unroll=True)
-        a_partner(1).wait_send()
+            running += c_in[i].astype(jnp.float32)
+        a_total[1, 0] = running
 
     @pl.when(h == 1)
     def _():
@@ -440,10 +442,10 @@
         kept = lax.fori_loop(1, 16, add, a_own[1, 1], unroll=True)
         for i in range(16):
             c_copy(i).wait_send()
+        a_partner(0).wait()
         a_partner(1).wait_recv()
         a_total[1, 1] = kept + a_last[1]
 
-    a_partner(0).wait()
     a_done = a_total[0, h] + a_last[0]
     b_done = a_total[1, h]
     o_ref[...] = jnp.concatenate([b_done[:, :BATCH], a_done, b_done[:, BATCH:]], axis=1)

time: 55.2 us -> 55.1 us (level)
  no operation moved by 1% of the time
where the time goes in v7:
time: 55.1 us; the launch traced here: 54.9 us
  Pallas kernels  54.3 us (99%)
  other arithmetic  0.62 us (1%)
    pallas_call x1, Pallas kernels, per_device(): pl.pallas_call(kernel, out_shape=pltpu.VMEM((32, Q), f32), in_specs=[pl.B...  54.3 us

profile of v7, /device:TPU:1, one launch (start us, length us, event | category | flops | bytes accessed | tf_op | source)
XLA Modules:
  0.0 54.9 jit_solution(4237641574502512627)
XLA Ops:
  0.0 54.3 %scores.1 = f32[32,256]{1,0:T(8,128)S(1)} custom-call(bf16[32,4096]{1,0:T(8,128)(2,1)} %bitcast.5, bf16[1024,4096]{1,0:T(8,128)(2,1)} %bitcast.3, bf16[4096,512]{1,0:T(8,128)(2,1)} %bitcast.4), custom_call_target="tpu_custom_call" | custom-call | tf_op jit(solution)/shard_map/scores/pallas_call | solution.py:457
  54.3 0.6 %broadcast_multiply_fusion = f32[32,256]{1,0:T(8,128)} fusion(f32[32,256]{1,0:T(8,128)S(1)} %scores.1), kind=kLoop, calls=%fused_computation | loop fusion | flops 8192 | bytes 65536 | tf_op jit(solution)/shard_map/mul | solution.py:498

commit v8 on v7

--- a/solution.py
+++ b/solution.py
@@ -303,8 +303,8 @@
 
             @pl.when((half == 1) & (h == 1))
             def _():
-                for m in (2, 3, 1, 0):
-                    c_copy(away * 4 + m).start()
+                for m in range(4):
+                    c_copy(away * 4 + (m + 4 - x) % 4).start()
 
             @pl.when((half == 0) | (h == 0))
             def _():

time: 55.1 us -> 55.1 us (level)
  no operation moved by 1% of the time
where the time goes in v8:
time: 55.1 us; the launch traced here: 54.9 us
  Pallas kernels  54.2 us (98%)
  other arithmetic  0.62 us (1%)
    pallas_call x1, Pallas kernels, per_device(): pl.pallas_call(kernel, out_shape=pltpu.VMEM((32, Q), f32), in_specs=[pl.B...  54.2 us

profile of v8, /device:TPU:1, one launch (start us, length us, event | category | flops | bytes accessed | tf_op | source)
XLA Modules:
  0.0 54.9 jit_solution(1863160326944013461)
XLA Ops:
  0.0 54.2 %scores.1 = f32[32,256]{1,0:T(8,128)S(1)} custom-call(bf16[32,4096]{1,0:T(8,128)(2,1)} %bitcast.5, bf16[1024,4096]{1,0:T(8,128)(2,1)} %bitcast.3, bf16[4096,512]{1,0:T(8,128)(2,1)} %bitcast.4), custom_call_target="tpu_custom_call" | custom-call | tf_op jit(solution)/shard_map/scores/pallas_call | solution.py:457
  54.3 0.6 %broadcast_multiply_fusion = f32[32,256]{1,0:T(8,128)} fusion(f32[32,256]{1,0:T(8,128)S(1)} %scores.1), kind=kLoop, calls=%fused_computation | loop fusion | flops 8192 | bytes 65536 | tf_op jit(solution)/shard_map/mul | solution.py:498
